TPU v7x, 512 devices: a whole 4x4x16 slice. The times are simulated.
512 devices in a mesh: seq: 64 (over x, z), head: 8 (over y, core).
Axes of the slice: x: 4, y: 4, z: 16, core: 2. Of those that a mesh axis runs over, the one named last changes fastest.
Arguments:
- tokens: bfloat16 [16384, 5376], P('seq', 'head'), may hold values from -6 to 6
- features: bfloat16 [512, 64, 1152], P('seq'), may hold values from -6 to 6
- starts: int32 [8], replicated, may hold values from 0 to 16128, as said below
- sources: int32 [8], replicated, may hold values from 0 to 56, as said below
- soft_gain: float32 [1152], replicated, may hold values from 0.25 to 1.75
- proj_weight: bfloat16 [1152, 5376], P(None, 'head'), may hold values from -0.1875 to 0.1875
- input_gain: float32 [5376], replicated, may hold values from 0.25 to 1.75
- query_weight: bfloat16 [5376, 2048], P('seq', 'head'), may hold values from -0.078125 to 0.078125
- key_weight: bfloat16 [5376, 1024], P('seq', 'head'), may hold values from -0.078125 to 0.078125
- value_weight: bfloat16 [5376, 1024], P('seq', 'head'), may hold values from -0.078125 to 0.078125
- query_gain: float32 [128], replicated, may hold values from 0.25 to 1.75
- key_gain: float32 [128], replicated, may hold values from 0.25 to 1.75
- out_weight: bfloat16 [2048, 5376], P('seq', 'head'), may hold values from -0.125 to 0.125
- post_gain: float32 [5376], P('head'), may hold values from 0.25 to 1.75
Outputs:
- layer_out: bfloat16 [16384, 5376], P('seq', 'head')
Inputs may be any that keep to these rules, and one draw needn't show every extreme that they name: Image i takes positions starts[i] to starts[i] + 255; the spans are in increasing order of i, do not intersect, and each crosses one boundary between sequence shards. Distinct multiples of 8; image i's patches fill feature rows sources[i] * 8 onward.
All inputs are finite; a program needn't handle non-finite values.
Results may differ from a plain program's by a relative error of at most 0.012.
Values may be sent and summed in bfloat16 or wider, within the bound.
No kernel may reach another device: no remote copies, remote signals or barrier semaphores. Data moves between devices by JAX's collectives and lax.ppermute only.
A program may use at most 64 MiB of HBM per device.

v0:
```python
import jax
import jax.numpy as jnp
from jax import lax
from jax.sharding import Mesh
from jax.sharding import PartitionSpec as P

D = 5376
HEAD_DIM = 128
WINDOW = 1024
PATCH_SIDE = 64
POOL = 4
IMG_TOK = 256
SEQ = ("x", "z")
HEAD = ("y", "core")
EPSILON = 1e-06
QUERY_SCALE = 168.0 ** (-0.5)
ROPE_BASE = 10000.0


def shifted(value, axis, steps):
    count = lax.axis_size(axis)
    leading, last = (max(0, -steps), min(count, count - steps))
    return lax.ppermute(value, axis, [(source, source + steps) for source in range(leading, last)])


def rms_scale(inputs, scale_gain):
    return (
        inputs * lax.rsqrt(jnp.mean(inputs * inputs, axis=-1, keepdims=True) + EPSILON) * scale_gain
    )


def rotate(inputs, positions):
    half_dim = inputs.shape[-1] // 2
    frequency = ROPE_BASE ** (-jnp.arange(half_dim, dtype=jnp.float32) * 2.0 / inputs.shape[-1])
    angles = positions.astype(jnp.float32)[:, None] * frequency[None, :]
    cosine = jnp.cos(angles)[:, None, :]
    sine_part = jnp.sin(angles)[:, None, :]
    first_half = inputs[..., :half_dim]
    second = inputs[..., half_dim:]
    return jnp.concatenate(
        [first_half * cosine - second * sine_part, second * cosine + first_half * sine_part],
        axis=-1,
    )


def image_of(positions, starts):
    inside = (positions[:, None] >= starts[None, :]) & (
        positions[:, None] < starts[None, :] + IMG_TOK
    )
    labels = jnp.arange(1, starts.shape[0] + 1, dtype=jnp.int32)
    return jnp.sum(jnp.where(inside, labels[None, :], 0), axis=1) - 1


def allowed_keys(query_pos, key_pos, starts, total_rows):
    query_img = image_of(query_pos, starts)
    key_img = image_of(key_pos, starts)
    inside = (key_pos >= 0) & (key_pos < total_rows)
    in_window = query_pos[:, None] - key_pos[None, :] < WINDOW
    causal = key_pos[None, :] <= query_pos[:, None]
    same_image = (query_img[:, None] == key_img[None, :]) & (query_img[:, None] >= 0)
    return inside[None, :] & in_window & (causal | same_image)


def attend(queries, key_rows, values, allowed):
    scores = jnp.einsum("qgrd,kgd->grqk", queries, key_rows, preferred_element_type=jnp.float32)
    scores = jnp.where(allowed[None, None], scores, -jnp.inf)
    row_max = jnp.max(scores, axis=-1, keepdims=True)
    weights = jnp.exp(scores - row_max)
    row_sum = jnp.sum(weights, axis=-1)
    mixed_heads = jnp.einsum(
        "grqk,kgd->qgrd", weights.astype(jnp.bfloat16), values, preferred_element_type=jnp.float32
    )
    return (mixed_heads / jnp.transpose(row_sum, (2, 0, 1))[..., None]).astype(jnp.bfloat16)


def exchange(value, axes, count):
    spread = jnp.broadcast_to(value[None], (count, *value.shape))
    return lax.all_to_all(spread, axes, 0, 0, tiled=True)


def body(
    tokens,
    features,
    starts,
    sources,
    soft_gain,
    proj_weight,
    input_gain,
    query_weight,
    key_weight,
    value_weight,
    query_gain,
    key_gain,
    out_weight,
    post_gain,
):
    tok_rows, width = tokens.shape
    x_count = lax.axis_size("x")
    z_count = lax.axis_size("z")
    head_count = lax.axis_size("y") * lax.axis_size("core")
    seq_count = x_count * z_count
    x_index = lax.axis_index("x")
    z_index = lax.axis_index("z")
    head_index = lax.axis_index(HEAD)
    seq_index = lax.axis_index(SEQ)
    total_rows = seq_count * tok_rows
    rows_in = query_weight.shape[0]
    rows_out = out_weight.shape[0]
    qkv_local = jnp.concatenate([query_weight, key_weight, value_weight], axis=1)
    qkv_x = lax.all_gather(qkv_local, "x", axis=0, tiled=True)
    qkv_zx = lax.all_gather(qkv_x, "z", axis=0, tiled=True)
    out_x = lax.all_gather(out_weight, "x", axis=0, tiled=True)
    out_zx = lax.all_gather(out_x, "z", axis=0, tiled=True)
    image_count = starts.shape[0]
    vis = features.shape[2]
    pooled_side = PATCH_SIDE // POOL
    pool_rows = features.shape[0] // POOL
    block_rows = pool_rows * pooled_side
    shards_each = pooled_side // pool_rows
    patch_grid = features.reshape(pool_rows, POOL, pooled_side, POOL, vis)
    pooled = jnp.sum(patch_grid, axis=(1, 3), dtype=jnp.float32).reshape(block_rows, vis) / (
        POOL * POOL
    )
    soft = rms_scale(pooled, soft_gain).astype(jnp.bfloat16)
    vis_part = vis // head_count
    soft_part = lax.dynamic_slice_in_dim(soft, head_index * vis_part, vis_part, 1)
    soft_z = exchange(soft_part, "z", z_count).reshape(z_count * block_rows, vis_part)
    frame_pos = (
        (jnp.arange(x_count, dtype=jnp.int32)[:, None] * z_count + z_index) * tok_rows
        + jnp.arange(tok_rows, dtype=jnp.int32)[None, :]
    ).reshape(-1)
    frame_image = image_of(frame_pos, starts)
    row_base = sources // shards_each * (block_rows * shards_each) - starts
    image_ids = jnp.arange(image_count, dtype=jnp.int32)
    frame_row = jnp.sum(
        jnp.where(frame_image[:, None] == image_ids[None, :], row_base[None, :], 0), axis=1
    )
    frame_row = jnp.where(frame_image >= 0, frame_row + frame_pos, -1)
    here = x_index * (z_count * block_rows) + jnp.arange(z_count * block_rows, dtype=jnp.int32)
    chosen = (frame_row[:, None] == here[None, :]).astype(jnp.bfloat16)
    chosen = chosen.reshape(x_count, tok_rows, z_count * block_rows)
    frames = jnp.einsum("sk,xps->xkp", soft_z, chosen, preferred_element_type=jnp.float32)
    frames = lax.all_to_all(frames.astype(jnp.bfloat16), "x", 0, 0, tiled=True)
    mine = jnp.sum(frames.astype(jnp.float32), axis=0).astype(jnp.bfloat16)
    soft_rows = exchange(mine, HEAD, head_count).reshape(vis, tok_rows)
    embedded = lax.dot_general(
        soft_rows, proj_weight, (((0,), (0,)), ((), ())), preferred_element_type=jnp.float32
    ).astype(jnp.bfloat16)
    my_pos = seq_index * tok_rows + jnp.arange(tok_rows, dtype=jnp.int32)
    my_image = image_of(my_pos, starts)
    residual = jnp.where((my_image >= 0)[:, None], embedded, tokens)
    whole = exchange(residual, HEAD, head_count).astype(jnp.float32)
    mean_square = jnp.sum(whole * whole, axis=(0, 2), keepdims=True) / D
    gains = input_gain.reshape(head_count, 1, width)
    normed = (whole * lax.rsqrt(mean_square + EPSILON) * gains).astype(jnp.bfloat16)
    qkv_weight = (
        qkv_zx.reshape(z_count, x_count, rows_in, -1)
        .transpose(1, 0, 2, 3)
        .reshape(head_count, width, -1)
    )
    qkv = jnp.einsum("hqk,hkn->qn", normed, qkv_weight, preferred_element_type=jnp.float32)
    kv_local = key_weight.shape[1] // HEAD_DIM
    group_size = query_weight.shape[1] // key_weight.shape[1]
    q_width = query_weight.shape[1]
    k_width = key_weight.shape[1]
    query_sum = qkv[:, :q_width]
    key_sum = qkv[:, q_width : q_width + k_width]
    value_sum = qkv[:, q_width + k_width :]
    queries = (
        rotate(
            rms_scale(query_sum.reshape(tok_rows, kv_local * group_size, HEAD_DIM), query_gain),
            my_pos,
        )
        * QUERY_SCALE
    )
    queries = queries.astype(jnp.bfloat16).reshape(tok_rows, kv_local, group_size, HEAD_DIM)
    own_keys = (
        rotate(rms_scale(key_sum.reshape(tok_rows, kv_local, HEAD_DIM), key_gain), my_pos)
        .astype(jnp.bfloat16)
        .reshape(tok_rows, k_width)
    )
    own = jnp.concatenate([own_keys, value_sum.astype(jnp.bfloat16)], axis=1)
    past_count = WINDOW // tok_rows
    pieces = [shifted(own, SEQ, step) for step in range(past_count, 0, -1)]
    pieces += [own, shifted(own, SEQ, -1)]
    window = jnp.concatenate(pieces, axis=0)
    key_pos = (seq_index - past_count) * tok_rows + jnp.arange(window.shape[0], dtype=jnp.int32)
    allowed = allowed_keys(my_pos, key_pos, starts, total_rows)
    attended = attend(
        queries,
        window[:, :k_width].reshape(-1, kv_local, HEAD_DIM),
        window[:, k_width:].reshape(-1, kv_local, HEAD_DIM),
        allowed,
    )
    attended = attended.reshape(tok_rows, kv_local * group_size * HEAD_DIM)
    heads_all = exchange(attended, HEAD, head_count)
    heads_weight = (
        out_zx.reshape(z_count, x_count, rows_out, width)
        .transpose(1, 0, 2, 3)
        .reshape(head_count, q_width, width)
    )
    projected = jnp.einsum(
        "hqk,hkn->qn", heads_all, heads_weight, preferred_element_type=jnp.float32
    )
    squares = jnp.sum(exchange(jnp.sum(projected * projected, axis=1), HEAD, head_count), axis=0)
    post = projected * lax.rsqrt(squares[:, None] / D + EPSILON) * post_gain
    return (residual.astype(jnp.float32) + post).astype(jnp.bfloat16)


def solution(mesh):
    split = Mesh(mesh.devices.reshape(4, 16, 4, 2), ("x", "z", "y", "core"))
    return jax.shard_map(
        body,
        mesh=split,
        in_specs=(
            P(SEQ, HEAD),
            P(SEQ, None, None),
            P(),
            P(),
            P(),
            P(None, HEAD),
            P(),
            P(SEQ, HEAD),
            P(SEQ, HEAD),
            P(SEQ, HEAD),
            P(),
            P(),
            P(SEQ, HEAD),
            P(HEAD),
        ),
        out_specs=P(SEQ, HEAD),
        check_vma=False,
    )
```

profile of v0, /device:TPU:2, one launch (start us, length us, event | category | flops | bytes accessed | tf_op | source)
XLA Modules:
  0.0 253.8 jit_solution(5185182241604811078)
XLA Ops:
  6.5 0.9 maximum_bitcast_fusion
  7.5 15.1 %all-gather = bf16[4,84,512]{2,1,0:T(8,128)(2,1)S(1)} all-gather(bf16[1,84,512]{2,1,0:T(8,128)(2,1)S(1)} %maximum_bitcast_fusion), channel_id=1, replica_groups=mesh['x'=4,'z'=16,'y'=4,'core'=2] {'x'}, dimensions={0}, use_global_device_ids=true | all-gather | bytes 430080 | tf_op jit(solution)/shard_map/all_gather | solution.py:110
  22.6 0.8 reshape.474
  23.5 3.3 %reshape.472 = f32[2,4,16,4,1152]{4,3,2,1,0:T(4,128)} reshape(bf16[8,64,1152]{2,1,0:T(8,128)(2,1)} %param.15) | data formatting | bytes 3538944 | tf_op jit(solution)/shard_map/convert_element_type | solution.py:121
  26.8 2.2 reduce_sum.132
  29.2 0.8 dynamic-slice
  30.1 0.7 broadcast_in_dim.78
  30.8 12.8 %all-to-all-start = ((bf16[16,32,144]{2,1,0:T(8,128)(2,1)}), bf16[16,32,144]{2,1,0:T(8,128)(2,1)S(1)}, u32[]{:S(2)}, u32[]{:S(2)}) async-start(bf16[16,32,144]{2,1,0:T(8,128)(2,1)} %broadcast_in_dim.78), calls=%async_computation | async-start | bytes 524288 | tf_op jit(solution)/shard_map/all_to_all | solution.py:78
  44.1 18.5 %all-to-all-done = bf16[16,32,144]{2,1,0:T(8,128)(2,1)S(1)} async-done(((bf16[16,32,144]{2,1,0:T(8,128)(2,1)}), bf16[16,32,144]{2,1,0:T(8,128)(2,1)S(1)}, u32[]{:S(2)}, u32[]{:S(2)}) %all-to-all-start) | async-done | bytes 147488 | tf_op jit(solution)/shard_map/all_to_all | solution.py:78
  62.6 0.6 fusion.25
  63.2 9.7 %all_to_all.31 = bf16[4,144,256]{2,1,0:T(8,128)(2,1)S(1)} all-to-all(bf16[4,144,256]{2,1,0:T(8,128)(2,1)S(1)} %fusion.25), channel_id=1, replica_groups=mesh['x'=4,'z'=16,'y'=4,'core'=2] {'x'}, dimensions={0} | all-to-all | bytes 589824 | tf_op jit(solution)/shard_map/all_to_all | solution.py:143
  73.0 0.8 broadcast_in_dim.79
  73.8 4.7 %all-to-all-start.2 = ((bf16[8,144,256]{2,1,0:T(8,128)(2,1)}), bf16[8,144,256]{2,1,0:T(8,128)(2,1)S(1)}, u32[]{:S(2)}, u32[]{:S(2)}) async-start(bf16[8,144,256]{2,1,0:T(8,128)(2,1)} %broadcast_in_dim.79), calls=%async_computation.2 | async-start | bytes 1179648 | tf_op jit(solution)/shard_map/all_to_all | solution.py:78
  78.6 10.9 %all-to-all-done.2 = bf16[8,144,256]{2,1,0:T(8,128)(2,1)S(1)} async-done(((bf16[8,144,256]{2,1,0:T(8,128)(2,1)}), bf16[8,144,256]{2,1,0:T(8,128)(2,1)S(1)}, u32[]{:S(2)}, u32[]{:S(2)}) %all-to-all-start.2) | async-done | bytes 589856 | tf_op jit(solution)/shard_map/all_to_all | solution.py:78
  89.6 0.6 fusion.24
  90.2 1.7 broadcast_in_dim.80
  91.9 4.6 %all-to-all-start.3 = ((bf16[8,256,672]{1,2,0:T(8,128)(2,1)}), bf16[8,256,672]{1,2,0:T(8,128)(2,1)}, u32[]{:S(2)}, u32[]{:S(2)}) async-start(bf16[8,256,672]{1,2,0:T(8,128)(2,1)} %broadcast_in_dim.80), calls=%async_computation.3 | async-start | bytes 5505024 | tf_op jit(solution)/shard_map/all_to_all | solution.py:78
  96.6 12.3 %all_gather.14 = bf16[128,672]{1,0:T(8,128)(2,1)} all-gather(bf16[32,672]{1,0:T(8,128)(2,1)S(1)} %copy-done.1), channel_id=1, replica_groups=mesh['x'=4,'z'=16,'y'=4,'core'=2] {'x'}, dimensions={0}, use_global_device_ids=true | all-gather | bytes 215040 | tf_op jit(solution)/shard_map/all_gather | solution.py:112
  109.7 1.4 fusion.17
  111.1 19.6 %all-to-all-done.3 = bf16[8,256,672]{1,2,0:T(8,128)(2,1)} async-done(((bf16[8,256,672]{1,2,0:T(8,128)(2,1)}), bf16[8,256,672]{1,2,0:T(8,128)(2,1)}, u32[]{:S(2)}, u32[]{:S(2)}) %all-to-all-start.3) | async-done | bytes 2752544 | tf_op jit(solution)/shard_map/all_to_all | solution.py:78
  130.7 2.5 fusion
  133.3 8.9 %reshape.466 = bf16[16,4,84,512]{3,2,1,0:T(8,128)(2,1)} reshape(bf16[5376,512]{1,0:T(8,128)(2,1)} %all-gather.4.cloned.1.call-done) | data formatting | bytes 11010048 | tf_op jit(solution)/shard_map/reshape | solution.py:157
  142.2 5.7 %copy.56 = bf16[4,16,84,512]{3,2,1,0:T(8,128)(2,1)} copy(bf16[4,16,84,512]{3,2,0,1:T(8,128)(2,1)} %bitcast.76) | data formatting | bytes 11010048 | tf_op jit(solution)/shard_map/transpose | solution.py:158
  147.9 8.9 %reshape.467 = bf16[8,672,512]{2,1,0:T(8,128)(2,1)} reshape(bf16[4,16,84,512]{3,2,1,0:T(8,128)(2,1)} %copy.56) | data formatting | bytes 11010048 | tf_op jit(solution)/shard_map/reshape | solution.py:159
  156.8 6.6 %fusion.18 = f32[256,512]{1,0:T(8,128)S(1)} fusion(bf16[8,672,512]{2,1,0:T(8,128)(2,1)} %reshape.467, bf16[8,256,672]{1,2,0:T(8,128)(2,1)} %all-to-all-done.3, f32[8,672]{1,0:T(8,128)S(1)} %mul.255, f32[256]{0:T(256)S(1)} %add_rsqrt_fusion.3), kind=kOutput, calls=%fused_computation.22 | convolution fusion | flops 1414791168 | bytes 8804352 | tf_op jit(solution)/shard_map/hqk,hkn->qn/dot_general | solution.py:161
  164.4 4.9 %collective-permute-start = (bf16[256,256]{1,0:T(8,128)(2,1)S(1)}, bf16[256,256]{1,0:T(8,128)(2,1)}, u32[]{:S(2)}, u32[]{:S(2)}) collective-permute-start(bf16[256,256]{1,0:T(8,128)(2,1)S(1)} %pad_maximum_fusion), channel_id=1, source_target_pairs={{0,32},{8,40},{16,48},{24,56},{32,64},{40,72},{48,80},{56,88},{64,... | collective-permute-start | bytes 393224 | tf_op jit(solution)/shard_map/ppermute | solution.py:23
  169.3 3.5 %collective-permute-start.1 = (bf16[256,256]{1,0:T(8,128)(2,1)S(1)}, bf16[256,256]{1,0:T(8,128)(2,1)}, u32[]{:S(2)}, u32[]{:S(2)}) collective-permute-start(bf16[256,256]{1,0:T(8,128)(2,1)S(1)} %pad_maximum_fusion), channel_id=1, source_target_pairs={{0,24},{8,32},{16,40},{24,48},{32,56},{40,64},{48,72},{56,80},{64,... | collective-permute-start | bytes 393224 | tf_op jit(solution)/shard_map/ppermute | solution.py:23
  172.7 3.1 %collective-permute-start.2 = (bf16[256,256]{1,0:T(8,128)(2,1)S(1)}, bf16[256,256]{1,0:T(8,128)(2,1)}, u32[]{:S(2)}, u32[]{:S(2)}) collective-permute-start(bf16[256,256]{1,0:T(8,128)(2,1)S(1)} %pad_maximum_fusion), channel_id=1, source_target_pairs={{0,16},{8,24},{16,32},{24,40},{32,48},{40,56},{48,64},{56,72},{64,... | collective-permute-start | bytes 393224 | tf_op jit(solution)/shard_map/ppermute | solution.py:23
  175.9 4.1 %collective-permute-start.3 = (bf16[256,256]{1,0:T(8,128)(2,1)S(1)}, bf16[256,256]{1,0:T(8,128)(2,1)}, u32[]{:S(2)}, u32[]{:S(2)}) collective-permute-start(bf16[256,256]{1,0:T(8,128)(2,1)S(1)} %pad_maximum_fusion), channel_id=1, source_target_pairs={{0,8},{8,16},{16,24},{24,32},{32,40},{40,48},{48,56},{56,64},{64,7... | collective-permute-start | bytes 393224 | tf_op jit(solution)/shard_map/ppermute | solution.py:23
  180.0 4.0 %collective-permute-start.4 = (bf16[256,256]{1,0:T(8,128)(2,1)S(1)}, bf16[256,256]{1,0:T(8,128)(2,1)}, u32[]{:S(2)}, u32[]{:S(2)}) collective-permute-start(bf16[256,256]{1,0:T(8,128)(2,1)S(1)} %pad_maximum_fusion), channel_id=1, source_target_pairs={{8,0},{16,8},{24,16},{32,24},{40,32},{48,40},{56,48},{64,56},{72,6... | collective-permute-start | bytes 393224 | tf_op jit(solution)/shard_map/ppermute | solution.py:23
  185.0 2.0 collective-permute-done
  187.0 0.9 constant_dynamic-update-slice_fusion.5
  187.9 11.0 %collective-permute-done.1 = bf16[256,256]{1,0:T(8,128)(2,1)} collective-permute-done((bf16[256,256]{1,0:T(8,128)(2,1)S(1)}, bf16[256,256]{1,0:T(8,128)(2,1)}, u32[]{:S(2)}, u32[]{:S(2)}) %collective-permute-start.1) | collective-permute-done | bytes 131104 | tf_op jit(solution)/shard_map/ppermute | solution.py:23
  198.9 0.9 constant_dynamic-update-slice_fusion.4
  199.8 4.6 %collective-permute-done.2 = bf16[256,256]{1,0:T(8,128)(2,1)} collective-permute-done((bf16[256,256]{1,0:T(8,128)(2,1)S(1)}, bf16[256,256]{1,0:T(8,128)(2,1)}, u32[]{:S(2)}, u32[]{:S(2)}) %collective-permute-start.2) | collective-permute-done | bytes 131104 | tf_op jit(solution)/shard_map/ppermute | solution.py:23
  204.4 0.9 constant_dynamic-update-slice_fusion.3
  205.3 3.1 %collective-permute-done.3 = bf16[256,256]{1,0:T(8,128)(2,1)} collective-permute-done((bf16[256,256]{1,0:T(8,128)(2,1)S(1)}, bf16[256,256]{1,0:T(8,128)(2,1)}, u32[]{:S(2)}, u32[]{:S(2)}) %collective-permute-start.3) | collective-permute-done | bytes 131104 | tf_op jit(solution)/shard_map/ppermute | solution.py:23
  208.5 0.9 constant_dynamic-update-slice_fusion.2
  209.4 0.9 constant_dynamic-update-slice_fusion
  210.3 0.7 fusion.60
  211.5 0.7 fusion.34
  212.2 1.1 broadcast_in_dim.90
  213.3 3.9 %all-to-all-start.4 = ((bf16[8,256,256]{2,1,0:T(8,128)(2,1)}), bf16[8,256,256]{2,1,0:T(8,128)(2,1)S(1)}, u32[]{:S(2)}, u32[]{:S(2)}) async-start(bf16[8,256,256]{2,1,0:T(8,128)(2,1)} %broadcast_in_dim.90), calls=%async_computation.4 | async-start | bytes 2097152 | tf_op jit(solution)/shard_map/all_to_all | solution.py:78
  217.2 3.8 %copy.62 = bf16[16,4,32,672]{3,2,0,1:T(8,128)(2,1)} copy(bf16[16,4,32,672]{3,2,1,0:T(8,128)(2,1)} %bitcast.77) | data formatting | bytes 5505024 | tf_op jit(solution)/shard_map/reshape | solution.py:198
  221.0 12.1 %all-to-all-done.4 = bf16[8,256,256]{2,1,0:T(8,128)(2,1)S(1)} async-done(((bf16[8,256,256]{2,1,0:T(8,128)(2,1)}), bf16[8,256,256]{2,1,0:T(8,128)(2,1)S(1)}, u32[]{:S(2)}, u32[]{:S(2)}) %all-to-all-start.4) | async-done | bytes 1048608 | tf_op jit(solution)/shard_map/all_to_all | solution.py:78
  233.1 4.1 %multiply_reduce_fusion = (f32[256]{0:T(256)S(1)}, f32[256,672]{0,1:T(8,128)}) fusion(bf16[8,256,256]{2,1,0:T(8,128)(2,1)S(1)} %all-to-all-done.4, bf16[8,256,672]{2,1,0:T(8,128)(2,1)} %bitcast.78), kind=kOutput, calls=%fused_computation.33 | convolution fusion | flops 704986880 | bytes 4490240 | tf_op jit(solution)/shard_map/hqk,hkn->qn/dot_general | solution.py:202
  237.2 7.7 %all_to_all.32 = f32[8,1,256]{2,1,0:T(1,128)S(1)} all-to-all(f32[8,1,256]{2,1,0:T(1,128)S(1)} %broadcast_in_dim.91), channel_id=1, replica_groups=mesh['x'=4,'z'=16,'y'=4,'core'=2] {'y','core'}, dimensions={0} | all-to-all | bytes 16384 | tf_op jit(solution)/shard_map/all_to_all | solution.py:78
  244.9 2.0 add_convert_fusion
  (74 shorter events, 4.1 us)
Async XLA Ops:
  6.5 83.0 %copy-start = (bf16[1152,672]{0,1:T(8,128)(2,1)S(1)}, bf16[1152,672]{0,1:T(8,128)(2,1)}, u32[]{:S(2)}) copy-start(bf16[1152,672]{0,1:T(8,128)(2,1)} %param.19) | copy-start | bytes 4644868
  6.5 126.7 %all-gather.4.cloned.1.call-start = ((), (), s32[]{:S(2)}) async-start(), calls=%async_computation.6 | async-start | bytes 5849088 | tf_op jit(solution)/shard_map/all_gather | solution.py:111
  23.5 20.3 %copy-start.3 = (s32[8]{0:T(128)S(1)}, s32[8]{0:T(128)}, u32[]{:S(2)}) copy-start(s32[8]{0:T(128)} %param.16) | copy-start | bytes 100
  23.5 20.3 %copy-start.7 = (s32[8]{0:T(128)S(1)}, s32[8]{0:T(128)}, u32[]{:S(2)}) copy-start(s32[8]{0:T(128)} %param.17) | copy-start | bytes 100
  29.0 60.5 %copy-start.8 = (bf16[256,672]{0,1:T(8,128)(2,1)S(1)}, bf16[256,672]{0,1:T(8,128)(2,1)}, u32[]{:S(2)}) copy-start(bf16[256,672]{0,1:T(8,128)(2,1)} %param.14) | copy-start | bytes 1032196
  30.8 31.8 %all-to-all-start = ((bf16[16,32,144]{2,1,0:T(8,128)(2,1)}), bf16[16,32,144]{2,1,0:T(8,128)(2,1)S(1)}, u32[]{:S(2)}, u32[]{:S(2)}) async-start(bf16[16,32,144]{2,1,0:T(8,128)(2,1)} %broadcast_in_dim.78), calls=%async_computation | async-start | bytes 524288 | tf_op jit(solution)/shard_map/all_to_all | solution.py:78
  73.8 15.7 %all-to-all-start.2 = ((bf16[8,144,256]{2,1,0:T(8,128)(2,1)}), bf16[8,144,256]{2,1,0:T(8,128)(2,1)S(1)}, u32[]{:S(2)}, u32[]{:S(2)}) async-start(bf16[8,144,256]{2,1,0:T(8,128)(2,1)} %broadcast_in_dim.79), calls=%async_computation.2 | async-start | bytes 1179648 | tf_op jit(solution)/shard_map/all_to_all | solution.py:78
  91.9 4.6 %copy-start.1 = (bf16[32,672]{1,0:T(8,128)(2,1)S(1)}, bf16[32,672]{1,0:T(8,128)(2,1)}, u32[]{:S(2)}) copy-start(bf16[32,672]{1,0:T(8,128)(2,1)} %param.26) | copy-start | bytes 129028
  91.9 16.9 %copy-start.2 = (f32[5376]{0:T(1024)S(1)}, f32[5376]{0:T(1024)}, u32[]{:S(2)}) copy-start(f32[5376]{0:T(1024)} %param.20) | copy-start | bytes 64516
  91.9 38.8 %all-to-all-start.3 = ((bf16[8,256,672]{1,2,0:T(8,128)(2,1)}), bf16[8,256,672]{1,2,0:T(8,128)(2,1)}, u32[]{:S(2)}, u32[]{:S(2)}) async-start(bf16[8,256,672]{1,2,0:T(8,128)(2,1)} %broadcast_in_dim.80), calls=%async_computation.3 | async-start | bytes 5505024 | tf_op jit(solution)/shard_map/all_to_all | solution.py:78
  96.5 120.7 %all-gather.6.cloned.1.call-start = ((), (), s32[]{:S(2)}) async-start(), calls=%async_computation.7 | async-start | bytes 3342336 | tf_op jit(solution)/shard_map/all_gather | solution.py:113
  156.8 6.8 %copy-start.5 = (f32[128]{0:T(128)S(1)}, f32[128]{0:T(128)}, u32[]{:S(2)}) copy-start(f32[128]{0:T(128)} %param.25) | copy-start | bytes 1540
  156.8 27.8 %copy-start.6 = (f32[128]{0:T(128)S(1)}, f32[128]{0:T(128)}, u32[]{:S(2)}) copy-start(f32[128]{0:T(128)} %param.24) | copy-start | bytes 1540
  164.4 22.6 %collective-permute-start = (bf16[256,256]{1,0:T(8,128)(2,1)S(1)}, bf16[256,256]{1,0:T(8,128)(2,1)}, u32[]{:S(2)}, u32[]{:S(2)}) collective-permute-start(bf16[256,256]{1,0:T(8,128)(2,1)S(1)} %pad_maximum_fusion), channel_id=1, source_target_pairs={{0,32},{8,40},{16,48},{24,56},{32,64},{40,72},{48,80},{56,88},{64,... | collective-permute-start | bytes 393224 | tf_op jit(solution)/shard_map/ppermute | solution.py:23
  169.3 29.6 %collective-permute-start.1 = (bf16[256,256]{1,0:T(8,128)(2,1)S(1)}, bf16[256,256]{1,0:T(8,128)(2,1)}, u32[]{:S(2)}, u32[]{:S(2)}) collective-permute-start(bf16[256,256]{1,0:T(8,128)(2,1)S(1)} %pad_maximum_fusion), channel_id=1, source_target_pairs={{0,24},{8,32},{16,40},{24,48},{32,56},{40,64},{48,72},{56,80},{64,... | collective-permute-start | bytes 393224 | tf_op jit(solution)/shard_map/ppermute | solution.py:23
  172.7 31.7 %collective-permute-start.2 = (bf16[256,256]{1,0:T(8,128)(2,1)S(1)}, bf16[256,256]{1,0:T(8,128)(2,1)}, u32[]{:S(2)}, u32[]{:S(2)}) collective-permute-start(bf16[256,256]{1,0:T(8,128)(2,1)S(1)} %pad_maximum_fusion), channel_id=1, source_target_pairs={{0,16},{8,24},{16,32},{24,40},{32,48},{40,56},{48,64},{56,72},{64,... | collective-permute-start | bytes 393224 | tf_op jit(solution)/shard_map/ppermute | solution.py:23
  175.9 32.6 %collective-permute-start.3 = (bf16[256,256]{1,0:T(8,128)(2,1)S(1)}, bf16[256,256]{1,0:T(8,128)(2,1)}, u32[]{:S(2)}, u32[]{:S(2)}) collective-permute-start(bf16[256,256]{1,0:T(8,128)(2,1)S(1)} %pad_maximum_fusion), channel_id=1, source_target_pairs={{0,8},{8,16},{16,24},{24,32},{32,40},{40,48},{48,56},{56,64},{64,7... | collective-permute-start | bytes 393224 | tf_op jit(solution)/shard_map/ppermute | solution.py:23
  180.0 29.4 %collective-permute-start.4 = (bf16[256,256]{1,0:T(8,128)(2,1)S(1)}, bf16[256,256]{1,0:T(8,128)(2,1)}, u32[]{:S(2)}, u32[]{:S(2)}) collective-permute-start(bf16[256,256]{1,0:T(8,128)(2,1)S(1)} %pad_maximum_fusion), channel_id=1, source_target_pairs={{8,0},{16,8},{24,16},{32,24},{40,32},{48,40},{56,48},{64,56},{72,6... | collective-permute-start | bytes 393224 | tf_op jit(solution)/shard_map/ppermute | solution.py:23
  213.3 19.8 %all-to-all-start.4 = ((bf16[8,256,256]{2,1,0:T(8,128)(2,1)}), bf16[8,256,256]{2,1,0:T(8,128)(2,1)S(1)}, u32[]{:S(2)}, u32[]{:S(2)}) async-start(bf16[8,256,256]{2,1,0:T(8,128)(2,1)} %broadcast_in_dim.90), calls=%async_computation.4 | async-start | bytes 2097152 | tf_op jit(solution)/shard_map/all_to_all | solution.py:78
  221.0 23.9 %copy-start.4 = (f32[672]{0:T(1024)S(1)}, f32[672]{0:T(1024)}, u32[]{:S(2)}) copy-start(f32[672]{0:T(1024)} %param.27) | copy-start | bytes 8068
Sparse Core Ops, SparseCore 0:
  23.6 93.3 all-gather.3
  119.0 91.8 all-gather.5
where the time goes:
time: 255 us; the launch traced here: 254 us
  waiting for transfers between devices  82 us (32%)
  starting transfers between devices  45.6 us (18%)
  blocking collectives  44.8 us (18%)
  local copies, waits for them, and re-layouts  41.8 us (16%)
  between operations  13.8 us (5%)
  matrix products  13.3 us (5%)
  other arithmetic  12.5 us (5%)
    all_to_all x4, waiting for transfers between devices, exchange(): return lax.all_to_all(spread, axes, 0, 0, tiled=True)  61.2 us
    all_to_all x4, starting transfers between devices, exchange(): return lax.all_to_all(spread, axes, 0, 0, tiled=True)  25.9 us
    ppermute x5, waiting for transfers between devices, shifted(): lax.ppermute(value, axis, [(source, source + steps) for source in range(l...  20.7 us
    ppermute x5, starting transfers between devices, shifted(): lax.ppermute(value, axis, [(source, source + steps) for source in range(l...  19.6 us
    all_gather x1, blocking collectives, body(): qkv_x = lax.all_gather(qkv_local, 'x', axis=0, tiled=True)  15.1 us
    all_gather x1, blocking collectives, body(): out_x = lax.all_gather(out_weight, 'x', axis=0, tiled=True)  12.3 us
    all_to_all x1, blocking collectives, body(): frames = lax.all_to_all(frames.astype(jnp.bfloat16), 'x', 0, 0, tiled=True)  9.7 us
    reshape x1, local copies, waits for them, and re-layouts, body(): qkv_zx.reshape(z_count, x_count, rows_in, -1).transpose(1, 0, 2, 3)  8.91 us
  transfers between devices with their start and end apart: 11, of which 8 were waited for; matrix products, arithmetic and copies ran while one was open for 24% of the time, Pallas kernels for 0%

commit v1 on v0

--- a/solution.py
+++ b/solution.py
@@ -108,7 +108,9 @@
     rows_out = out_weight.shape[0]
     qkv_local = jnp.concatenate([query_weight, key_weight, value_weight], axis=1)
     qkv_x = lax.all_gather(qkv_local, "x", axis=0, tiled=True)
-    qkv_zx = lax.all_gather(qkv_x, "z", axis=0, tiled=True)
+    qkv_zx = jnp.concatenate(
+        lax.all_to_all(jnp.stack([qkv_x] * lax.axis_size("z")), "z", 0, 0), axis=0
+    )
     out_x = lax.all_gather(out_weight, "x", axis=0, tiled=True)
     out_zx = lax.all_gather(out_x, "z", axis=0, tiled=True)
     image_count = starts.shape[0]

time: 255 us -> 505 us (1.98)
  waiting for transfers between devices: 82 us -> 324 us
  starting transfers between devices: 45.6 us -> 58.2 us
    all_to_all x0 -> x1, waiting for transfers between devices: none -> 253 us  [body(): lax.all_to_all(jnp.stack([qkv_x] * lax.axis_size('z')), 'z', 0, 0)]
    ppermute x5, waiting for transfers between devices: 20.7 us -> 7.73 us  [shifted(): lax.ppermute(value, axis, [(source, source + steps) for source in range(l...]
    reshape x1 -> x0, local copies, waits for them, and re-layouts: 8.91 us -> none  [body(): qkv_zx.reshape(z_count, x_count, rows_in, -1).transpose(1, 0, 2, 3)]
    all_to_all x0 -> x1, starting transfers between devices: none -> 6.07 us  [body(): lax.all_to_all(jnp.stack([qkv_x] * lax.axis_size('z')), 'z', 0, 0)]
    all_to_all x0 -> x1, local copies, waits for them, and re-layouts: none -> 5.65 us  [body(): lax.all_to_all(jnp.stack([qkv_x] * lax.axis_size('z')), 'z', 0, 0)]
  transfers between devices with their start and end apart: 11 -> 11, of which waited for: 8 -> 8; matrix products, arithmetic and copies ran while one was open for 24% -> 9% of each run, Pallas kernels for 0% -> 0%
where the time goes in v1:
time: 505 us; the launch traced here: 504 us
  waiting for transfers between devices  324 us (64%)
  starting transfers between devices  58.2 us (12%)
  blocking collectives  42 us (8%)
  local copies, waits for them, and re-layouts  40.8 us (8%)
  between operations  13.9 us (3%)
  matrix products  13.2 us (3%)
  other arithmetic  11.6 us (2%)
    all_to_all x1, waiting for transfers between devices, body(): lax.all_to_all(jnp.stack([qkv_x] * lax.axis_size('z')), 'z', 0, 0)  253 us
    all_to_all x4, waiting for transfers between devices, exchange(): return lax.all_to_all(spread, axes, 0, 0, tiled=True)  63.1 us
    all_to_all x4, starting transfers between devices, exchange(): return lax.all_to_all(spread, axes, 0, 0, tiled=True)  27.8 us
    ppermute x5, starting transfers between devices, shifted(): lax.ppermute(value, axis, [(source, source + steps) for source in range(l...  24.4 us
    all_gather x1, blocking collectives, body(): out_x = lax.all_gather(out_weight, 'x', axis=0, tiled=True)  12.4 us
    all_gather x1, blocking collectives, body(): qkv_x = lax.all_gather(qkv_local, 'x', axis=0, tiled=True)  11.9 us
  transfers between devices with their start and end apart: 11, of which 8 were waited for; matrix products, arithmetic and copies ran while one was open for 9% of the time, Pallas kernels for 0%

profile of v1, /device:TPU:2, one launch (start us, length us, event | category | flops | bytes accessed | tf_op | source)
XLA Modules:
  0.0 503.7 jit_solution(17134125720107044580)
XLA Ops:
  6.5 3.4 reshape.470
  9.9 2.2 reduce_sum.132
  12.4 0.8 dynamic-slice
  13.3 0.7 broadcast_in_dim.78
  14.0 15.2 %all-to-all-start = ((bf16[16,32,144]{2,1,0:T(8,128)(2,1)}), bf16[16,32,144]{2,1,0:T(8,128)(2,1)S(1)}, u32[]{:S(2)}, u32[]{:S(2)}) async-start(bf16[16,32,144]{2,1,0:T(8,128)(2,1)} %broadcast_in_dim.78), calls=%async_computation | async-start | bytes 524288 | tf_op jit(solution)/shard_map/all_to_all | solution.py:78
  29.6 17.9 %all-to-all-done = bf16[16,32,144]{2,1,0:T(8,128)(2,1)S(1)} async-done(((bf16[16,32,144]{2,1,0:T(8,128)(2,1)}), bf16[16,32,144]{2,1,0:T(8,128)(2,1)S(1)}, u32[]{:S(2)}, u32[]{:S(2)}) %all-to-all-start) | async-done | bytes 147488 | tf_op jit(solution)/shard_map/all_to_all | solution.py:78
  47.6 0.6 fusion.25
  48.2 10.0 %all_to_all.36 = bf16[4,144,256]{2,1,0:T(8,128)(2,1)S(1)} all-to-all(bf16[4,144,256]{2,1,0:T(8,128)(2,1)S(1)} %fusion.25), channel_id=1, replica_groups=mesh['x'=4,'z'=16,'y'=4,'core'=2] {'x'}, dimensions={0} | all-to-all | bytes 589824 | tf_op jit(solution)/shard_map/all_to_all | solution.py:145
  58.3 0.8 broadcast_in_dim.79
  59.1 4.5 all-to-all-start.2
  63.7 10.9 %all-to-all-done.2 = bf16[8,144,256]{2,1,0:T(8,128)(2,1)S(1)} async-done(((bf16[8,144,256]{2,1,0:T(8,128)(2,1)}), bf16[8,144,256]{2,1,0:T(8,128)(2,1)S(1)}, u32[]{:S(2)}, u32[]{:S(2)}) %all-to-all-start.2) | async-done | bytes 589856 | tf_op jit(solution)/shard_map/all_to_all | solution.py:78
  74.7 0.6 fusion.24
  75.3 1.7 broadcast_in_dim.80
  77.0 4.5 all-to-all-start.3
  81.6 11.9 %all-gather = bf16[4,84,512]{2,1,0:T(8,128)(2,1)S(1)} all-gather(bf16[1,84,512]{2,1,0:T(8,128)(2,1)S(1)} %maximum_bitcast_fusion), channel_id=1, replica_groups=mesh['x'=4,'z'=16,'y'=4,'core'=2] {'x'}, dimensions={0}, use_global_device_ids=true | all-gather | bytes 430080 | tf_op jit(solution)/shard_map/all_gather | solution.py:110
  93.6 22.2 %all-to-all-done.3 = bf16[8,256,672]{1,2,0:T(8,128)(2,1)} async-done(((bf16[8,256,672]{1,2,0:T(8,128)(2,1)}), bf16[8,256,672]{1,2,0:T(8,128)(2,1)}, u32[]{:S(2)}, u32[]{:S(2)}) %all-to-all-start.3) | async-done | bytes 2752544 | tf_op jit(solution)/shard_map/all_to_all | solution.py:78
  115.8 3.0 stack.2
  118.8 6.1 %all-to-all-start.4 = ((bf16[16,336,512]{2,1,0:T(8,128)(2,1)}), bf16[16,336,512]{2,1,0:T(8,128)(2,1)}, u32[]{:S(2)}, u32[]{:S(2)}) async-start(bf16[16,336,512]{2,1,0:T(8,128)(2,1)} %stack.2), calls=%async_computation.4 | async-start | bytes 11010048 | tf_op jit(solution)/shard_map/all_to_all | solution.py:112
  124.9 12.4 %all_gather.10 = bf16[128,672]{1,0:T(8,128)(2,1)} all-gather(bf16[32,672]{1,0:T(8,128)(2,1)S(1)} %copy-done.1), channel_id=1, replica_groups=mesh['x'=4,'z'=16,'y'=4,'core'=2] {'x'}, dimensions={0}, use_global_device_ids=true | all-gather | bytes 215040 | tf_op jit(solution)/shard_map/all_gather | solution.py:114
  138.2 1.4 fusion.17
  139.6 2.5 fusion
  142.2 253.0 %all-to-all-done.4 = bf16[16,336,512]{2,1,0:T(8,128)(2,1)} async-done(((bf16[16,336,512]{2,1,0:T(8,128)(2,1)}), bf16[16,336,512]{2,1,0:T(8,128)(2,1)}, u32[]{:S(2)}, u32[]{:S(2)}) %all-to-all-start.4) | async-done | bytes 5505056 | tf_op jit(solution)/shard_map/all_to_all | solution.py:112
  395.2 5.7 %copy.59 = bf16[16,336,512]{2,0,1:T(8,128)(2,1)S(1)} copy(bf16[16,336,512]{2,1,0:T(8,128)(2,1)} %all-to-all-done.4) | data formatting | bytes 11010048 | tf_op jit(solution)/shard_map/all_to_all | solution.py:112
  400.8 5.7 %copy.60 = bf16[4,16,84,512]{3,2,1,0:T(8,128)(2,1)} copy(bf16[4,16,84,512]{3,1,2,0:T(8,128)(2,1)S(1)} %bitcast.78) | data formatting | bytes 11010048 | tf_op jit(solution)/shard_map/transpose | solution.py:160
  406.5 8.9 %reshape.465 = bf16[8,672,512]{2,1,0:T(8,128)(2,1)} reshape(bf16[4,16,84,512]{3,2,1,0:T(8,128)(2,1)} %copy.60) | data formatting | bytes 11010048 | tf_op jit(solution)/shard_map/reshape | solution.py:161
  415.4 6.5 %fusion.18 = f32[256,512]{1,0:T(8,128)S(1)} fusion(bf16[8,672,512]{2,1,0:T(8,128)(2,1)} %reshape.465, bf16[8,256,672]{1,2,0:T(8,128)(2,1)} %all-to-all-done.3, f32[8,672]{1,0:T(8,128)S(1)} %mul.255, f32[256]{0:T(256)S(1)} %add_rsqrt_fusion.3), kind=kOutput, calls=%fused_computation.22 | convolution fusion | flops 1414791168 | bytes 8804352 | tf_op jit(solution)/shard_map/hqk,hkn->qn/dot_general | solution.py:163
  422.9 6.8 %collective-permute-start = (bf16[256,256]{1,0:T(8,128)(2,1)S(1)}, bf16[256,256]{1,0:T(8,128)(2,1)}, u32[]{:S(2)}, u32[]{:S(2)}) collective-permute-start(bf16[256,256]{1,0:T(8,128)(2,1)S(1)} %pad_maximum_fusion), channel_id=1, source_target_pairs={{0,32},{8,40},{16,48},{24,56},{32,64},{40,72},{48,80},{56,88},{64,... | collective-permute-start | bytes 393224 | tf_op jit(solution)/shard_map/ppermute | solution.py:23
  429.7 6.2 %collective-permute-start.1 = (bf16[256,256]{1,0:T(8,128)(2,1)S(1)}, bf16[256,256]{1,0:T(8,128)(2,1)}, u32[]{:S(2)}, u32[]{:S(2)}) collective-permute-start(bf16[256,256]{1,0:T(8,128)(2,1)S(1)} %pad_maximum_fusion), channel_id=1, source_target_pairs={{0,24},{8,32},{16,40},{24,48},{32,56},{40,64},{48,72},{56,80},{64,... | collective-permute-start | bytes 393224 | tf_op jit(solution)/shard_map/ppermute | solution.py:23
  435.9 3.2 collective-permute-start.2
  439.1 3.6 collective-permute-start.3
  442.7 4.5 collective-permute-start.4
  448.3 0.9 constant_dynamic-update-slice_fusion.5
  449.2 2.3 collective-permute-done.1
  451.4 0.9 constant_dynamic-update-slice_fusion.4
  452.3 3.9 collective-permute-done.2
  456.2 0.9 constant_dynamic-update-slice_fusion.3
  457.1 1.6 collective-permute-done.3
  458.7 0.9 constant_dynamic-update-slice_fusion.2
  459.7 0.9 constant_dynamic-update-slice_fusion
  460.6 0.7 fusion.60
  461.7 0.7 fusion.34
  462.5 1.1 broadcast_in_dim.90
  463.6 3.6 all-to-all-start.5
  467.2 3.8 copy.66
  471.0 12.0 %all-to-all-done.5 = bf16[8,256,256]{2,1,0:T(8,128)(2,1)S(1)} async-done(((bf16[8,256,256]{2,1,0:T(8,128)(2,1)}), bf16[8,256,256]{2,1,0:T(8,128)(2,1)S(1)}, u32[]{:S(2)}, u32[]{:S(2)}) %all-to-all-start.5) | async-done | bytes 1048608 | tf_op jit(solution)/shard_map/all_to_all | solution.py:78
  483.0 4.1 multiply_reduce_fusion
  487.1 7.7 %all_to_all.37 = f32[8,1,256]{2,1,0:T(1,128)S(1)} all-to-all(f32[8,1,256]{2,1,0:T(1,128)S(1)} %broadcast_in_dim.91), channel_id=1, replica_groups=mesh['x'=4,'z'=16,'y'=4,'core'=2] {'y','core'}, dimensions={0} | all-to-all | bytes 16384 | tf_op jit(solution)/shard_map/all_to_all | solution.py:78
  494.8 2.0 add_convert_fusion
  (80 shorter events, 4.1 us)
Async XLA Ops:
  6.5 68.1 %copy-start = (bf16[1152,672]{0,1:T(8,128)(2,1)S(1)}, bf16[1152,672]{0,1:T(8,128)(2,1)}, u32[]{:S(2)}) copy-start(bf16[1152,672]{0,1:T(8,128)(2,1)} %param.19) | copy-start | bytes 4644868
  6.5 22.8 %copy-start.6 = (s32[8]{0:T(128)S(1)}, s32[8]{0:T(128)}, u32[]{:S(2)}) copy-start(s32[8]{0:T(128)} %param.16) | copy-start | bytes 100
  6.5 22.8 %copy-start.10 = (s32[8]{0:T(128)S(1)}, s32[8]{0:T(128)}, u32[]{:S(2)}) copy-start(s32[8]{0:T(128)} %param.17) | copy-start | bytes 100
  12.2 62.5 %copy-start.11 = (bf16[256,672]{0,1:T(8,128)(2,1)S(1)}, bf16[256,672]{0,1:T(8,128)(2,1)}, u32[]{:S(2)}) copy-start(bf16[256,672]{0,1:T(8,128)(2,1)} %param.14) | copy-start | bytes 1032196
  14.0 33.6 %all-to-all-start = ((bf16[16,32,144]{2,1,0:T(8,128)(2,1)}), bf16[16,32,144]{2,1,0:T(8,128)(2,1)S(1)}, u32[]{:S(2)}, u32[]{:S(2)}) async-start(bf16[16,32,144]{2,1,0:T(8,128)(2,1)} %broadcast_in_dim.78), calls=%async_computation | async-start | bytes 524288 | tf_op jit(solution)/shard_map/all_to_all | solution.py:78
  59.1 15.5 %all-to-all-start.2 = ((bf16[8,144,256]{2,1,0:T(8,128)(2,1)}), bf16[8,144,256]{2,1,0:T(8,128)(2,1)S(1)}, u32[]{:S(2)}, u32[]{:S(2)}) async-start(bf16[8,144,256]{2,1,0:T(8,128)(2,1)} %broadcast_in_dim.79), calls=%async_computation.2 | async-start | bytes 1179648 | tf_op jit(solution)/shard_map/all_to_all | solution.py:78
  77.0 4.6 copy-start.2
  77.0 4.6 copy-start.4
  77.0 4.6 copy-start.5
  77.0 38.8 %all-to-all-start.3 = ((bf16[8,256,672]{1,2,0:T(8,128)(2,1)}), bf16[8,256,672]{1,2,0:T(8,128)(2,1)}, u32[]{:S(2)}, u32[]{:S(2)}) async-start(bf16[8,256,672]{1,2,0:T(8,128)(2,1)} %broadcast_in_dim.80), calls=%async_computation.3 | async-start | bytes 5505024 | tf_op jit(solution)/shard_map/all_to_all | solution.py:78
  118.8 6.1 %copy-start.1 = (bf16[32,672]{1,0:T(8,128)(2,1)S(1)}, bf16[32,672]{1,0:T(8,128)(2,1)}, u32[]{:S(2)}) copy-start(bf16[32,672]{1,0:T(8,128)(2,1)} %param.26) | copy-start | bytes 129028
  118.8 18.6 %copy-start.3 = (f32[5376]{0:T(1024)S(1)}, f32[5376]{0:T(1024)}, u32[]{:S(2)}) copy-start(f32[5376]{0:T(1024)} %param.20) | copy-start | bytes 64516
  118.8 276.4 %all-to-all-start.4 = ((bf16[16,336,512]{2,1,0:T(8,128)(2,1)}), bf16[16,336,512]{2,1,0:T(8,128)(2,1)}, u32[]{:S(2)}, u32[]{:S(2)}) async-start(bf16[16,336,512]{2,1,0:T(8,128)(2,1)} %stack.2), calls=%async_computation.4 | async-start | bytes 11010048 | tf_op jit(solution)/shard_map/all_to_all | solution.py:112
  124.9 342.3 %all-gather.3.cloned.1.call-start = ((), (), s32[]{:S(2)}) async-start(), calls=%async_computation.7 | async-start | bytes 3342336 | tf_op jit(solution)/shard_map/all_gather | solution.py:115
  415.4 6.7 %copy-start.8 = (f32[128]{0:T(128)S(1)}, f32[128]{0:T(128)}, u32[]{:S(2)}) copy-start(f32[128]{0:T(128)} %param.25) | copy-start | bytes 1540
  415.4 32.6 %copy-start.9 = (f32[128]{0:T(128)S(1)}, f32[128]{0:T(128)}, u32[]{:S(2)}) copy-start(f32[128]{0:T(128)} %param.24) | copy-start | bytes 1540
  422.9 25.4 %collective-permute-start = (bf16[256,256]{1,0:T(8,128)(2,1)S(1)}, bf16[256,256]{1,0:T(8,128)(2,1)}, u32[]{:S(2)}, u32[]{:S(2)}) collective-permute-start(bf16[256,256]{1,0:T(8,128)(2,1)S(1)} %pad_maximum_fusion), channel_id=1, source_target_pairs={{0,32},{8,40},{16,48},{24,56},{32,64},{40,72},{48,80},{56,88},{64,... | collective-permute-start | bytes 393224 | tf_op jit(solution)/shard_map/ppermute | solution.py:23
  429.7 21.7 %collective-permute-start.1 = (bf16[256,256]{1,0:T(8,128)(2,1)S(1)}, bf16[256,256]{1,0:T(8,128)(2,1)}, u32[]{:S(2)}, u32[]{:S(2)}) collective-permute-start(bf16[256,256]{1,0:T(8,128)(2,1)S(1)} %pad_maximum_fusion), channel_id=1, source_target_pairs={{0,24},{8,32},{16,40},{24,48},{32,56},{40,64},{48,72},{56,80},{64,... | collective-permute-start | bytes 393224 | tf_op jit(solution)/shard_map/ppermute | solution.py:23
  435.9 20.3 %collective-permute-start.2 = (bf16[256,256]{1,0:T(8,128)(2,1)S(1)}, bf16[256,256]{1,0:T(8,128)(2,1)}, u32[]{:S(2)}, u32[]{:S(2)}) collective-permute-start(bf16[256,256]{1,0:T(8,128)(2,1)S(1)} %pad_maximum_fusion), channel_id=1, source_target_pairs={{0,16},{8,24},{16,32},{24,40},{32,48},{40,56},{48,64},{56,72},{64,... | collective-permute-start | bytes 393224 | tf_op jit(solution)/shard_map/ppermute | solution.py:23
  439.1 19.6 %collective-permute-start.3 = (bf16[256,256]{1,0:T(8,128)(2,1)S(1)}, bf16[256,256]{1,0:T(8,128)(2,1)}, u32[]{:S(2)}, u32[]{:S(2)}) collective-permute-start(bf16[256,256]{1,0:T(8,128)(2,1)S(1)} %pad_maximum_fusion), channel_id=1, source_target_pairs={{0,8},{8,16},{16,24},{24,32},{32,40},{40,48},{48,56},{56,64},{64,7... | collective-permute-start | bytes 393224 | tf_op jit(solution)/shard_map/ppermute | solution.py:23
  442.7 16.9 %collective-permute-start.4 = (bf16[256,256]{1,0:T(8,128)(2,1)S(1)}, bf16[256,256]{1,0:T(8,128)(2,1)}, u32[]{:S(2)}, u32[]{:S(2)}) collective-permute-start(bf16[256,256]{1,0:T(8,128)(2,1)S(1)} %pad_maximum_fusion), channel_id=1, source_target_pairs={{8,0},{16,8},{24,16},{32,24},{40,32},{48,40},{56,48},{64,56},{72,6... | collective-permute-start | bytes 393224 | tf_op jit(solution)/shard_map/ppermute | solution.py:23
  463.6 19.4 %all-to-all-start.5 = ((bf16[8,256,256]{2,1,0:T(8,128)(2,1)}), bf16[8,256,256]{2,1,0:T(8,128)(2,1)S(1)}, u32[]{:S(2)}, u32[]{:S(2)}) async-start(bf16[8,256,256]{2,1,0:T(8,128)(2,1)} %broadcast_in_dim.90), calls=%async_computation.5 | async-start | bytes 2097152 | tf_op jit(solution)/shard_map/all_to_all | solution.py:78
  471.0 23.8 %copy-start.7 = (f32[672]{0:T(1024)S(1)}, f32[672]{0:T(1024)}, u32[]{:S(2)}) copy-start(f32[672]{0:T(1024)} %param.27) | copy-start | bytes 8068
Sparse Core Ops, SparseCore 0:
  137.5 248.6 all-gather.2
